TPU v7x, 32 devices: a whole 2x2x4 slice. The times are simulated.
32 devices in a mesh: groups: 2 (over x), seq: 16 (over z, y, core).
Axes of the slice: x: 2, y: 2, z: 4, core: 2. Of those that a mesh axis runs over, the one named last changes fastest.
Arguments:
- tokens: bfloat16 [4096, 8192], P(('groups', 'seq')), parts along dimension 0, may hold values from -6 to 6
- request_adapters: int32 [32, 4], P(('groups', 'seq')), parts along dimension 0, may hold values from 0 to 1023
- prompt_token_count: int32 [32, 4], P(('groups', 'seq')), parts along dimension 0, may hold values from 1 to 48, 128 in all within a row
- adapter_slot_index: int32 [1024], replicated, may hold values from 0 to 1023, each once
- down_factor_shard: bfloat16 [16, 512, 65536], P('seq'), may hold values from -0.0625 to 0.0625
- up_factor_shard: bfloat16 [16, 512, 4096], P('seq'), may hold values from -0.75 to 0.75
- shared_key_weight: bfloat16 [8192, 512], P('seq'), may hold values from -0.0625 to 0.0625
Outputs:
- keys: bfloat16 [4096, 512], P(('groups', 'seq')), parts along dimension 0
There are 2 independent parts, one for each index of `groups`. A program takes and returns all parts, laid end to end along the dimension named above; an argument that names none is the same for every part. Nothing has to cross between parts.
Inputs may be any that keep to these rules, and one draw needn't show every extreme that they name: `prompt_token_count`: the counts of one device sum to 128. `adapter_slot_index`: each slot once.
All inputs are finite; a program needn't handle non-finite values.
Results may differ from a plain program's by a relative error of at most 0.0043.
Values may be sent and summed in bfloat16 or wider, within the bound.
A program may use at most 256 MiB of HBM per device.

v0:
```python
import math

import jax
import jax.numpy as jnp
from jax import lax
from jax.sharding import PartitionSpec as P

KEY_FEATURES = 512
ADAPTER_RANK = 64
OWNER_GROUPS = 2


def members(counts_row, row_count, req_count):
    seg_ends = jnp.cumsum(counts_row)
    positions = jnp.arange(row_count)
    owner_req = jnp.sum((positions[:, None] >= seg_ends[None, :]).astype(jnp.int32), axis=1)
    return owner_req[:, None] == jnp.arange(req_count)[None, :]


def on_device(
    tokens,
    request_adapters,
    prompt_token_count,
    adapter_slot_index,
    down_factor_shard,
    up_factor_shard,
    shared_key_weight,
):
    seq_count = lax.axis_size("seq")
    tok_rows = tokens.shape[0]
    feat_count = tokens.shape[1]
    req_count = request_adapters.shape[1]
    group_size = seq_count // OWNER_GROUPS
    stripe = feat_count // group_size
    owner_portion = down_factor_shard.shape[1]
    my_group = lax.axis_index("seq") // group_size
    down_factor_store = down_factor_shard[0]
    up_factor_store = up_factor_shard[0]
    my_slots = jnp.take(adapter_slot_index, request_adapters[0])
    member = members(prompt_token_count[0], tok_rows, req_count)
    all_slots, all_counts = (
        lax.all_gather(my_slots[None, :], "seq", axis=0, tiled=True),
        lax.all_gather(prompt_token_count, "seq", axis=0, tiled=True),
    )
    slot_group = my_slots // owner_portion
    row_group = jnp.sum(jnp.where(member, slot_group[None, :], 0), axis=1)
    split_rows = tokens.reshape(tok_rows, 1, group_size, stripe)
    owner_mask = row_group[:, None] == jnp.arange(OWNER_GROUPS)[None, :]
    send = jnp.where(owner_mask[:, :, None, None], split_rows, jnp.zeros((), tokens.dtype))
    send = send.reshape(tok_rows, seq_count, stripe)
    arrived = lax.all_to_all(send, "seq", split_axis=1, concat_axis=0, tiled=True)
    pieces = arrived.reshape(seq_count, tok_rows, stripe)
    source_total = tok_rows * lax.axis_size("seq") // tok_rows
    per_step = math.gcd(source_total, 16)

    def block_terms(step_index):
        block_first = step_index * per_step
        source_ids = block_first + jnp.arange(per_step)
        rows_block = lax.dynamic_slice_in_dim(pieces, block_first, per_step, 0)
        slots_block = jnp.take(all_slots, source_ids, axis=0)
        counts_block = jnp.take(all_counts, source_ids, axis=0)
        offset = jnp.clip(slots_block - my_group * owner_portion, 0, owner_portion - 1)
        panels = jnp.take(down_factor_store, offset.reshape(-1), axis=0)
        panels = panels.reshape(per_step, req_count, stripe, ADAPTER_RANK)
        member_block = jax.vmap(lambda row: members(row, tok_rows, req_count))(counts_block)
        terms = jnp.einsum("jtc,jqcr->jtqr", rows_block, panels, preferred_element_type=jnp.float32)
        picked = jnp.sum(jnp.where(member_block[:, :, :, None], terms, jnp.float32(0.0)), axis=2)
        return picked.reshape(per_step * tok_rows, ADAPTER_RANK)

    blocks = lax.map(block_terms, jnp.arange(source_total // per_step))
    shrunk = lax.psum_scatter(
        blocks.reshape(tok_rows * lax.axis_size("seq"), ADAPTER_RANK),
        "seq",
        scatter_dimension=0,
        tiled=True,
    )
    offset = all_slots - my_group * owner_portion
    inside = (offset >= 0) & (offset < owner_portion)
    picked = jnp.take(up_factor_store, jnp.clip(offset, 0, owner_portion - 1), axis=0)
    send_b = jnp.where(inside[..., None], picked, jnp.zeros((), up_factor_store.dtype))
    got_b = lax.all_to_all(send_b, "seq", split_axis=0, concat_axis=0, tiled=True)
    halves_b = jnp.sum(got_b.reshape(OWNER_GROUPS, group_size, req_count, got_b.shape[2]), axis=0)
    panels_b = halves_b.transpose(1, 0, 2).reshape(req_count * ADAPTER_RANK, KEY_FEATURES)
    shrunk_b = shrunk.astype(jnp.bfloat16)
    spread = jnp.where(member[:, :, None], shrunk_b[:, None, :], jnp.zeros((), jnp.bfloat16))
    spread = spread.reshape(tok_rows, req_count * ADAPTER_RANK)
    delta = jnp.dot(spread, panels_b, preferred_element_type=jnp.float32)
    base = jnp.dot(
        tokens,
        lax.all_gather(shared_key_weight, "seq", axis=0, tiled=True),
        preferred_element_type=jnp.float32,
    )
    return (base + delta).astype(jnp.bfloat16)


def solution(mesh):
    in_specs = (
        P(("groups", "seq"), None),
        P(("groups", "seq"), None),
        P(("groups", "seq"), None),
        P(),
        P("seq", None, None),
        P("seq", None, None),
        P("seq", None),
    )
    out_specs = P(("groups", "seq"), None)
    return jax.shard_map(
        on_device, mesh=mesh, in_specs=in_specs, out_specs=out_specs, check_vma=False
    )
```

profile of v0, /device:TPU:0, one launch (start us, length us, event | category | flops | bytes accessed | tf_op | source)
XLA Modules:
  0.0 365.1 jit_solution(16372809531670993714)
XLA Ops:
  6.5 0.7 fusion.4
  7.8 0.7 fusion.6
  8.5 0.8 reduce-window.8
  9.5 1.8 copy.54
  11.3 2.2 bitcast_select_fusion
  13.6 7.4 %all-to-all-start = ((bf16[128,16,1024]{2,0,1:T(8,128)(2,1)}), bf16[128,16,1024]{2,0,1:T(8,128)(2,1)}, u32[]{:S(2)}, u32[]{:S(2)}) async-start(bf16[128,16,1024]{2,0,1:T(8,128)(2,1)} %bitcast_select_fusion), calls=%async_computation | async-start | bytes 8388608 | tf_op jit(solution)/shard_map/all_to_all | solution.py:51
  21.1 83.8 %all-gather.1 = s32[16,1,4]{2,1,0:T(1,128)S(1)} all-gather(s32[1,1,4]{2,1,0:T(1,128)S(1)} %bitcast.61), channel_id=1, replica_groups=mesh['groups'=2,'seq'=16] {'seq'}, dimensions={0}, use_global_device_ids=true | all-gather | bytes 272 | tf_op jit(solution)/shard_map/all_gather | solution.py:42
  105.8 21.2 %gather_fusion.1 = bf16[64,65536]{1,0:T(8,128)(2,1)} fusion(bf16[512,65536]{1,0:T(8,128)(2,1)} %bitcast.15, s32[1024]{0:T(1024)S(1)} %pad_clamp_fusion.1), kind=kCustom, calls=%fused_computation.3 | custom fusion | bytes 16777472 | tf_op jit(solution)/shard_map/while/body/eval_jaxpr/jit(_take)/gather | solution.py:63
  127.0 18.2 %gather.23 = bf16[16,4,1024,64]{3,2,1,0:T(8,128)(2,1)} reshape(bf16[64,65536]{1,0:T(8,128)(2,1)} %gather_fusion.1) | data formatting | bytes 16777216 | tf_op jit(solution)/shard_map/while/body/eval_jaxpr/jit(_take)/gather | solution.py:63
  145.2 14.2 %broadcast_select_fusion = bf16[16,4,1024,64]{3,2,1,0:T(8,128)(2,1)} fusion(bf16[16,4,1024,64]{3,2,1,0:T(8,128)(2,1)} %gather.23, pred[16,4]{1,0:T(8,128)(4,1)S(1)} %get-tuple-element.34), kind=kLoop, calls=%fused_computation.5 | loop fusion | flops 4194304 | bytes 16777280 | tf_op jit(solution)/shard_map/while/body/eval_jaxpr/jit(_take)/select_n | solution.py:63
  159.4 15.9 %copy.45 = bf16[16,4,1024,64]{2,3,1,0:T(8,128)(2,1)} copy(bf16[16,4,1024,64]{3,2,1,0:T(8,128)(2,1)} %broadcast_select_fusion) | data formatting | bytes 16777216 | tf_op jit(solution)/shard_map/while/body/eval_jaxpr/jit(_take)/select_n | solution.py:63
  175.2 37.8 %all-gather = s32[16,1,4]{2,1,0:T(1,128)S(1)} all-gather(s32[1,1,4]{2,1,0:T(1,128)S(1)} %bitcast.63), channel_id=1, replica_groups=mesh['groups'=2,'seq'=16] {'seq'}, dimensions={0}, use_global_device_ids=true | all-gather | bytes 272 | tf_op jit(solution)/shard_map/all_gather | solution.py:43
  214.0 7.0 %fusion = f32[16,128,256]{1,2,0:S(1)} fusion(bf16[16,1024,256]{1,2,0:T(8,128)(2,1)} %bitcast.51, bf16[128,16,1024]{2,0,1:T(8,128)(2,1)} %all-to-all-done), kind=kOutput, calls=%fused_computation.6 | convolution fusion | flops 1073741824 | bytes 14680064
  221.4 0.9 copy_bitcast_fusion.1
  222.3 0.7 all-gather.4.cloned.1.call-update
  223.1 4.2 %gather_fusion.2 = bf16[64,4096]{1,0:T(8,128)(2,1)S(1)} fusion(bf16[512,4096]{1,0:T(8,128)(2,1)} %bitcast.55, s32[1024]{0:T(1024)S(1)} %pad_clamp_fusion), kind=kCustom, calls=%fused_computation.4 | custom fusion | bytes 1048832 | tf_op jit(solution)/shard_map/jit(_take)/gather | solution.py:79
  227.6 1.3 select_select_fusion
  228.9 3.6 all-to-all-start.1
  232.5 14.4 %all-to-all-done.1 = bf16[16,4,4096]{2,1,0:T(4,128)(2,1)S(1)} async-done(((bf16[16,4,4096]{2,1,0:T(4,128)(2,1)}), bf16[16,4,4096]{2,1,0:T(4,128)(2,1)S(1)}, u32[]{:S(2)}, u32[]{:S(2)}) %all-to-all-start.1) | async-done | bytes 524320 | tf_op jit(solution)/shard_map/all_to_all | solution.py:81
  247.7 28.6 %reduce-scatter.2.cloned.1.call-done = f32[128,64]{0,1:T(8,128)} async-done(((f32[2048,64]{0,1:T(8,128)}), f32[128,64]{0,1:T(8,128)}) %reduce-scatter.2.cloned.1.call-update) | async-done | bytes 32784 | tf_op jit(solution)/shard_map/reduce_scatter | solution.py:71
  276.3 0.8 convert_element_type.17
  277.0 75.6 %all-gather.4.cloned.1.call-done = bf16[8192,512]{1,0:T(8,128)(2,1)} async-done(((bf16[512,512]{1,0:T(8,128)(2,1)}), bf16[8192,512]{1,0:T(8,128)(2,1)}) %all-gather.4.cloned.1.call-update) | async-done | bytes 8388624 | tf_op jit(solution)/shard_map/all_gather | solution.py:90
  352.6 4.8 %fusion.8 = f32[128,512]{1,0:T(8,128)S(1)} fusion(bf16[128,8192]{1,0:T(8,128)(2,1)S(1)} %copy-done.2, bf16[8192,512]{1,0:T(8,128)(2,1)} %all-gather.4.cloned.1.call-done), kind=kOutput, calls=%fused_computation.49 | convolution fusion | flops 1073741824 | bytes 10747904 | tf_op jit(solution)/shard_map/dot_general | solution.py:88
  357.4 0.9 fusion.2
  (43 shorter events, 4.3 us)
Async XLA Ops:
  6.5 0.7 copy-start
  13.6 200.5 %all-to-all-start = ((bf16[128,16,1024]{2,0,1:T(8,128)(2,1)}), bf16[128,16,1024]{2,0,1:T(8,128)(2,1)}, u32[]{:S(2)}, u32[]{:S(2)}) async-start(bf16[128,16,1024]{2,0,1:T(8,128)(2,1)} %bitcast_select_fusion), calls=%async_computation | async-start | bytes 8388608 | tf_op jit(solution)/shard_map/all_to_all | solution.py:51
  21.0 255.3 %reduce-scatter.2.cloned.1.call-start = ((), (), s32[]{:S(2)}) async-start(), calls=%async_computation.4 | async-start | bytes 557056 | tf_op jit(solution)/shard_map/reduce_scatter | solution.py:71
  159.4 15.9 %copy-start.3 = (s32[1,4]{1,0:T(1,128)S(1)}, s32[1,4]{1,0:T(1,128)}, u32[]{:S(2)}) copy-start(s32[1,4]{1,0:T(1,128)} %param.11) | copy-start | bytes 52
  222.3 130.3 %all-gather.4.cloned.1.call-start = ((), (), s32[]{:S(2)}) async-start(), calls=%async_computation.3 | async-start | bytes 8912896 | tf_op jit(solution)/shard_map/all_gather | solution.py:90
  223.1 129.5 %copy-start.2 = (bf16[128,8192]{1,0:T(8,128)(2,1)S(1)}, bf16[128,8192]{1,0:T(8,128)(2,1)}, u32[]{:S(2)}) copy-start(bf16[128,8192]{1,0:T(8,128)(2,1)} %param.9) | copy-start | bytes 6291460
  228.9 18.0 %all-to-all-start.1 = ((bf16[16,4,4096]{2,1,0:T(4,128)(2,1)}), bf16[16,4,4096]{2,1,0:T(4,128)(2,1)S(1)}, u32[]{:S(2)}, u32[]{:S(2)}) async-start(bf16[16,4,4096]{2,1,0:T(4,128)(2,1)} %select_select_fusion), calls=%async_computation.2 | async-start | bytes 1048576 | tf_op jit(solution)/shard_map/all_to_all | solution.py:81
  352.6 5.7 %copy-start.1 = (s32[1024]{0:T(1024)S(1)}, s32[1024]{0:T(1024)}, u32[]{:S(2)}) copy-start(s32[1024]{0:T(1024)} %param.12) | copy-start | bytes 12292
Sparse Core Ops, SparseCore 0:
  222.4 53.8 reduce-scatter.1
  278.7 73.9 all-gather.3
where the time goes:
time: 366 us; the launch traced here: 365 us
  blocking collectives  122 us (33%)
  waiting for transfers between devices  119 us (33%)
  local copies, waits for them, and re-layouts  64.8 us (18%)
  other arithmetic  22.2 us (6%)
  between operations  13.6 us (4%)
  matrix products  12.6 us (3%)
  starting transfers between devices  11.1 us (3%)
    all_gather x1, blocking collectives, on_device(): lax.all_gather(my_slots[None, :], 'seq', axis=0, tiled=True)  83.8 us
    all_gather x1, waiting for transfers between devices, on_device(): lax.all_gather(shared_key_weight, 'seq', axis=0, tiled=True)  75.6 us
    gather x2, local copies, waits for them, and re-layouts, block_terms(): panels = jnp.take(down_factor_store, offset.reshape(-1), axis=0)  39.3 us
    all_gather x1, blocking collectives, on_device(): lax.all_gather(prompt_token_count, 'seq', axis=0, tiled=True)  37.8 us
    reduce_scatter x1, waiting for transfers between devices, on_device(): lax.psum_scatter(blocks.reshape(tok_rows * lax.axis_size('seq'), ADAPTER_...  28.6 us
    select_n x1, local copies, waits for them, and re-layouts, block_terms(): panels = jnp.take(down_factor_store, offset.reshape(-1), axis=0)  15.9 us
    all_to_all x1, waiting for transfers between devices, on_device(): lax.all_to_all(send_b, 'seq', split_axis=0, concat_axis=0, tiled=True)  14.4 us
    select_n x2, other arithmetic, block_terms(): panels = jnp.take(down_factor_store, offset.reshape(-1), axis=0)  14.2 us
  transfers between devices with their start and end apart: 4, of which 3 were waited for; matrix products, arithmetic and copies ran while one was open for 22% of the time, Pallas kernels for 0%

commit v1 on v0

v1 whole, which is shorter than its diff:
```python
import jax
import jax.numpy as jnp
from jax import lax
from jax.sharding import PartitionSpec as P

KEY_FEATURES = 512
ADAPTER_RANK = 64
OWNER_GROUPS = 2


def running(counts):
    at = jnp.arange(counts.shape[0])
    return jnp.sum(jnp.where(at[None, :] <= at[:, None], counts[None, :], 0), axis=1)


def request_of(ends, length):
    return jnp.sum((jnp.arange(length)[:, None] >= ends[None, :]).astype(jnp.int32), axis=1)


def on_device(
    tokens,
    request_adapters,
    prompt_token_count,
    adapter_slot_index,
    down_factor_shard,
    up_factor_shard,
    shared_key_weight,
):
    n = lax.axis_size("seq")
    rows, feats = tokens.shape
    reqs = request_adapters.shape[1]
    g = n // OWNER_GROUPS
    stripe = feats // g
    slots_here = down_factor_shard.shape[1]
    me = lax.axis_index("seq")
    mine = me // g
    halves = [list(range(h * g, h * g + g)) for h in range(OWNER_GROUPS)]
    mirror = [(j, (j + g) % n) for j in range(n)]

    def exchange(x):
        return lax.all_to_all(x, "seq", 0, 0, axis_index_groups=halves, tiled=True)

    facts = jnp.concatenate([request_adapters, prompt_token_count], axis=1)
    facts = lax.all_gather(facts, ("groups", "seq"), axis=0, tiled=True)
    tokens, shared_key_weight, facts = lax.optimization_barrier((tokens, shared_key_weight, facts))
    every_slot = jnp.take(adapter_slot_index, facts[:, :reqs])
    every_count = facts[:, reqs:]

    home = (jnp.arange(every_slot.shape[0]) // g) % OWNER_GROUPS
    crossing = jnp.where(every_slot // slots_here != home[:, None], every_count, 0)
    most = jnp.max(jnp.sum(crossing.reshape(-1, g * reqs), axis=1))

    first = lax.axis_index("groups") * n
    slots = lax.dynamic_slice_in_dim(every_slot, first, n, 0)
    counts = lax.dynamic_slice_in_dim(every_count, first, n, 0)

    half_rows = exchange(tokens.reshape(rows, g, stripe).transpose(1, 0, 2))

    even = [(2 * m, m) for m in range(g)] + [(2 * m + 1, g + m) for m in range(g)]
    odd = [(2 * m + 1, m) for m in range(g)] + [(2 * m, g + m) for m in range(g)]
    w_a = lax.ppermute(shared_key_weight, "seq", even)
    w_b = lax.ppermute(shared_key_weight, "seq", odd)
    w_lo = jnp.where(mine == 0, w_a, w_b)
    w_hi = jnp.where(mine == 0, w_b, w_a)

    offset = slots - mine * slots_here
    inside = (offset >= 0) & (offset < slots_here)
    offset = jnp.clip(offset, 0, slots_here - 1)
    picked_b = jnp.take(up_factor_shard[0], offset, axis=0)
    send_b = jnp.where(inside[..., None], picked_b, jnp.zeros((), picked_b.dtype))
    got_b = lax.all_to_all(send_b, "seq", 0, 0, tiled=True)

    own_at, far_at = mine * g, (1 - mine) * g
    offset_own = lax.dynamic_slice_in_dim(offset, own_at, g, 0).reshape(-1)
    offset_far = lax.dynamic_slice_in_dim(offset, far_at, g, 0).reshape(-1)
    panels_own = jnp.take(down_factor_shard[0], offset_own, axis=0)
    panels_far = jnp.take(down_factor_shard[0], offset_far, axis=0)

    own_counts = lax.dynamic_slice_in_dim(counts, own_at, g, 0)
    far_counts = lax.dynamic_slice_in_dim(counts, far_at, g, 0)
    own_inside = lax.dynamic_slice_in_dim(inside, own_at, g, 0)
    far_inside = lax.dynamic_slice_in_dim(inside, far_at, g, 0)
    total = g * rows

    own_flat = own_counts.reshape(-1)
    leaves = ~own_inside.reshape(-1)
    own_ends = running(own_flat)
    out_ends = running(jnp.where(leaves, own_flat, 0))
    row_req = request_of(own_ends, total)
    is_req = row_req[:, None] == jnp.arange(g * reqs)[None, :]
    shift = jnp.where(leaves, out_ends - own_ends, 2 * total)
    place = jnp.arange(total) + jnp.sum(jnp.where(is_req, shift[None, :], 0), axis=1)
    stays = is_req & own_inside.reshape(-1)[None, :]
    far_ends = running(jnp.where(far_inside, far_counts, 0).reshape(-1))

    def with_room(room):
        def branch(half_rows, w_lo, w_hi, panels_own, panels_far, place, stays, far_ends):
            flat = half_rows.reshape(total, stripe)
            chosen = place[None, :] == jnp.arange(room)[:, None]
            packed = jnp.dot(
                chosen.astype(jnp.bfloat16), flat, preferred_element_type=jnp.float32
            ).astype(jnp.bfloat16)
            came = lax.ppermute(packed, "seq", mirror)

            depth = w_lo.shape[0]
            base = jnp.dot(flat[:, :depth], w_lo, preferred_element_type=jnp.float32)
            base = base + jnp.dot(flat[:, depth:], w_hi, preferred_element_type=jnp.float32)
            base = exchange(base.astype(jnp.bfloat16).reshape(g, rows, KEY_FEATURES))
            base = jnp.sum(base.astype(jnp.float32), axis=0)

            p_own = panels_own.reshape(g, reqs, stripe, ADAPTER_RANK)
            keep = stays.reshape(g, rows, g, reqs)
            keep = jnp.sum(
                jnp.where(jnp.eye(g, dtype=bool)[:, None, :, None], keep, False), axis=2
            ).astype(bool)
            terms = jnp.einsum(
                "jtc,jqcr->jtqr", half_rows, p_own, preferred_element_type=jnp.float32
            )
            own = jnp.sum(jnp.where(keep[..., None], terms, 0.0), axis=2)

            p_far = panels_far.reshape(g * reqs, stripe, ADAPTER_RANK)
            step = room if room * g * reqs * ADAPTER_RANK <= (1 << 22) else rows
            req = request_of(far_ends, room)

            def far_terms(rows_in, req_in):
                terms = jnp.einsum(
                    "tc,qcr->tqr", rows_in, p_far, preferred_element_type=jnp.float32
                )
                hit = req_in[:, None] == jnp.arange(g * reqs)[None, :]
                return jnp.sum(jnp.where(hit[..., None], terms, 0.0), axis=1)

            if step == room:
                far = far_terms(came, req)
            else:
                far = lax.map(
                    lambda args: far_terms(*args),
                    (came.reshape(-1, step, stripe), req.reshape(-1, step)),
                ).reshape(room, ADAPTER_RANK)
            back = lax.ppermute(far, "seq", mirror)
            back = jnp.dot(
                chosen.astype(jnp.float32).T, back, precision=lax.Precision.HIGHEST
            )
            shrunk = own + back.reshape(g, rows, ADAPTER_RANK)
            shrunk = jnp.sum(exchange(shrunk), axis=0)
            return base, shrunk

        return branch

    unit = total // 16
    rooms = [unit * k for k in (8, 9, 10, 11, 12, 16)]
    which = sum((most > room).astype(jnp.int32) for room in rooms[:-1])
    base, shrunk = lax.switch(
        which,
        [with_room(room) for room in rooms],
        half_rows, w_lo, w_hi, panels_own, panels_far, place, stays, far_ends,
    )

    halves_b = jnp.sum(got_b.reshape(OWNER_GROUPS, g, reqs, got_b.shape[2]), axis=0)
    panels_b = halves_b.transpose(1, 0, 2).reshape(reqs * ADAPTER_RANK, KEY_FEATURES)
    member = request_of(running(prompt_token_count[0]), rows)[:, None] == jnp.arange(reqs)[None, :]
    shrunk_b = shrunk.astype(jnp.bfloat16)
    spread = jnp.where(member[:, :, None], shrunk_b[:, None, :], jnp.zeros((), jnp.bfloat16))
    spread = spread.reshape(rows, reqs * ADAPTER_RANK)
    delta = jnp.dot(spread, panels_b, preferred_element_type=jnp.float32)
    return (base + delta).astype(jnp.bfloat16)


def solution(mesh):
    in_specs = (
        P(("groups", "seq"), None),
        P(("groups", "seq"), None),
        P(("groups", "seq"), None),
        P(),
        P("seq", None, None),
        P("seq", None, None),
        P("seq", None),
    )
    out_specs = P(("groups", "seq"), None)
    return jax.shard_map(
        on_device, mesh=mesh, in_specs=in_specs, out_specs=out_specs, check_vma=False
    )
```

time: 366 us -> 265 us (0.72)
  waiting for transfers between devices: 119 us -> 38.1 us
  blocking collectives: 122 us -> 43 us
  local copies, waits for them, and re-layouts: 64.8 us -> 89.3 us
  loops' own time: 0 us -> 23.6 us
  starting transfers between devices: 11.1 us -> 24.4 us
  between operations: 13.6 us -> 3.83 us
  other arithmetic: 22.2 us -> 27.9 us
  matrix products: 12.6 us -> 17.4 us
    all_gather x2 -> x1, blocking collectives: 122 us -> 43 us  [on_device(): facts = lax.all_gather(facts, ('groups', 'seq'), axis=0, tiled=True)]
    all_gather x1 -> x0, waiting for transfers between devices: 75.6 us -> none  [on_device(): lax.all_gather(shared_key_weight, 'seq', axis=0, tiled=True)]
    reshape x3 -> x9, local copies, waits for them, and re-layouts: 1.09 us -> 41.3 us  [the longest x2 18.9 us: branch(): p_own = panels_own.reshape(g, reqs, stripe, ADAPTER_RANK)]
    reduce_scatter x1 -> x0, waiting for transfers between devices: 28.6 us -> none  [on_device(): lax.psum_scatter(blocks.reshape(tok_rows * lax.axis_size('seq'), ADAPTER_...]
    another operation x0 -> x1, loops' own time: none -> 23.6 us  [on_device(): lax.switch(which, [with_room(room) for room in rooms], half_rows, w_lo, w...]
    ppermute x0 -> x4, waiting for transfers between devices: none -> 21.1 us  [the longest x1 11 us: branch(): back = lax.ppermute(far, 'seq', mirror)]
    select_n x1 -> x0, local copies, waits for them, and re-layouts: 15.9 us -> none  [block_terms(): panels = jnp.take(down_factor_store, offset.reshape(-1), axis=0)]
    gather x7 -> x6, local copies, waits for them, and re-layouts: 45.5 us -> 33.3 us  [the longest x1 14.8 us: on_device(): panels_far = jnp.take(down_factor_shard[0], offset_far, axis=0)]
  transfers between devices with their start and end apart: 4 -> 8, of which waited for: 3 -> 4; matrix products, arithmetic and copies ran while one was open for 22% -> 38% of each run, Pallas kernels for 0% -> 0%
where the time goes in v1:
time: 265 us; the launch traced here: 268 us
  local copies, waits for them, and re-layouts  89.3 us (34%)
  blocking collectives  43 us (16%)
  waiting for transfers between devices  38.1 us (14%)
  other arithmetic  27.9 us (11%)
  starting transfers between devices  24.4 us (9%)
  loops' own time  23.6 us (9%)
  matrix products  17.4 us (7%)
  between operations  3.83 us (1%)
    all_gather x1, blocking collectives, on_device(): facts = lax.all_gather(facts, ('groups', 'seq'), axis=0, tiled=True)  43 us
    another operation x1, loops' own time, on_device(): lax.switch(which, [with_room(room) for room in rooms], half_rows, w_lo, w...  23.6 us
    reshape x2, local copies, waits for them, and re-layouts, branch(): p_own = panels_own.reshape(g, reqs, stripe, ADAPTER_RANK)  18.9 us
    reshape x2, local copies, waits for them, and re-layouts, branch(): p_far = panels_far.reshape(g * reqs, stripe, ADAPTER_RANK)  18.9 us
    gather x1, local copies, waits for them, and re-layouts, on_device(): panels_far = jnp.take(down_factor_shard[0], offset_far, axis=0)  14.8 us
    gather x1, local copies, waits for them, and re-layouts, on_device(): panels_own = jnp.take(down_factor_shard[0], offset_own, axis=0)  13.2 us
    all_to_all x1, waiting for transfers between devices, on_device(): got_b = lax.all_to_all(send_b, 'seq', 0, 0, tiled=True)  11.9 us
    ppermute x1, waiting for transfers between devices, branch(): back = lax.ppermute(far, 'seq', mirror)  11 us
  transfers between devices with their start and end apart: 8, of which 4 were waited for; matrix products, arithmetic and copies ran while one was open for 38% of the time, Pallas kernels for 0%

profile of v1, /device:TPU:0, one launch (start us, length us, event | category | flops | bytes accessed | tf_op | source)
XLA Modules:
  0.0 267.6 jit_solution(5508284656836467019)
XLA Ops:
  0.8 43.0 %all-gather = s32[32,1,8]{2,1,0:T(1,128)S(1)} all-gather(s32[1,1,8]{2,1,0:T(1,128)S(1)} %add_bitcast_fusion), channel_id=1, replica_groups=mesh['groups'=2,'seq'=16] {'groups','seq'}, dimensions={0}, use_global_device_ids=true | all-gather | bytes 1056 | tf_op jit(solution)/shard_map/all_gather | solution.py:44
  45.4 4.1 %gather_fusion.1 = bf16[64,4096]{1,0:T(8,128)(2,1)S(1)} fusion(bf16[512,4096]{1,0:T(8,128)(2,1)} %bitcast.236, s32[1024]{0:T(1024)S(1)} %pad_clamp_fusion), kind=kCustom, calls=%fused_computation.3 | custom fusion | bytes 1048832 | tf_op jit(solution)/shard_map/jit(_take)/gather | solution.py:69
  50.9 3.6 %all-to-all-start.13 = ((bf16[16,4,4096]{2,1,0:T(4,128)(2,1)}), bf16[16,4,4096]{2,1,0:T(4,128)(2,1)S(1)}, u32[]{:S(2)}, u32[]{:S(2)}) async-start(bf16[16,4,4096]{2,1,0:T(4,128)(2,1)} %select_select_fusion), calls=%async_computation.13 | async-start | bytes 1048576 | tf_op jit(solution)/shard_map/all_to_all | solution.py:71
  57.0 11.9 %all-to-all-done.13 = bf16[16,4,4096]{2,1,0:T(4,128)(2,1)S(1)} async-done(((bf16[16,4,4096]{2,1,0:T(4,128)(2,1)}), bf16[16,4,4096]{2,1,0:T(4,128)(2,1)S(1)}, u32[]{:S(2)}, u32[]{:S(2)}) %all-to-all-start.13) | async-done | bytes 524320 | tf_op jit(solution)/shard_map/all_to_all | solution.py:71
  69.7 3.6 %all-to-all-start.12 = ((bf16[8,128,1024]{1,2,0:T(8,128)(2,1)}), bf16[8,128,1024]{1,2,0:T(8,128)(2,1)S(1)}, u32[]{:S(2)}, u32[]{:S(2)}) async-start(bf16[8,128,1024]{1,2,0:T(8,128)(2,1)} %bitcast.201), calls=%async_computation.12 | async-start | bytes 4194304 | tf_op jit(solution)/shard_map/all_to_all | solution.py:41
  75.0 4.0 %collective-permute-start.13 = (bf16[512,512]{1,0:T(8,128)(2,1)}, bf16[512,512]{1,0:T(8,128)(2,1)S(1)}, u32[]{:S(2)}, u32[]{:S(2)}) collective-permute-start(bf16[512,512]{1,0:T(8,128)(2,1)} %param.21), channel_id=1, source_target_pairs={{1,0},{3,1},{5,2},{7,3},{9,4},{11,5},{13,6},{15,7},{0,8},{2,9},{4,... | collective-permute-start | bytes 1572872 | tf_op jit(solution)/shard_map/ppermute | solution.py:62
  84.0 13.2 %gather_fusion.2 = bf16[32,65536]{1,0:T(8,128)(2,1)} fusion(bf16[512,65536]{1,0:T(8,128)(2,1)} %bitcast.52, s32[1024]{0:T(1024)S(1)} %pad_clamp_fusion.2), kind=kCustom, calls=%fused_computation.clone | custom fusion | bytes 8388736 | tf_op jit(solution)/shard_map/jit(_take)/gather | solution.py:76
  97.1 14.8 %gather_fusion.3 = bf16[32,65536]{1,0:T(8,128)(2,1)} fusion(bf16[512,65536]{1,0:T(8,128)(2,1)} %bitcast.52, s32[1024]{0:T(1024)S(1)} %pad_clamp_fusion.1), kind=kCustom, calls=%fused_computation.1.clone | custom fusion | bytes 8388736 | tf_op jit(solution)/shard_map/jit(_take)/gather | solution.py:77
  121.8 142.9 %conditional.1 = (bf16[128,64]{0,1:T(8,128)(2,1)S(1)}, f32[128,512]{1,0:T(8,128)}) conditional(s32[]{:T(128)} %clamp.18, (s32[]{:T(128)}, bf16[512,512]{1,0:T(8,128)(2,1)S(1)}, bf16[512,512]{1,0:T(8,128)(2,1)S(1)}, bf16[8,128,1024]{1,2,0:T(8,128)(2,1)S(1)}, s32[1024,32]{1,0:T(8,128)}, ...), branch_computations={%region_4.16_spmd, %region_15.27_spmd, %region_26.38_spmd, %region... | conditional | flops 8873371648 | bytes 169005152 | solution.py:152
  144.5 2.6 copy.177
  151.9 4.5 %fusion.58 = bf16[768,1024]{1,0:T(8,128)(2,1)} fusion(bf16[1024,1024]{1,0:T(8,128)(2,1)} %bitcast.214, s32[1024]{0:T(1024)S(1)} %add.120), kind=kOutput, calls=%fused_computation.172 | convolution fusion | flops 1612185600 | bytes 3674112 | tf_op jit(solution)/shard_map/cond/branch_4_fun/dot_general | solution.py:100
  156.4 4.2 %collective-permute-start.8 = (bf16[768,1024]{1,0:T(8,128)(2,1)}, bf16[768,1024]{1,0:T(8,128)(2,1)}, u32[]{:S(2)}, u32[]{:S(2)}) collective-permute-start(bf16[768,1024]{1,0:T(8,128)(2,1)} %fusion.58), channel_id=1, source_target_pairs={{0,8},{1,9},{2,10},{3,11},{4,12},{5,13},{6,14},{7,15},{8,0},{9,1},... | collective-permute-start | bytes 4718600 | tf_op jit(solution)/shard_map/cond/branch_4_fun/ppermute | solution.py:103
  164.8 3.7 %all-to-all-start.8 = ((bf16[8,128,512]{1,2,0:T(8,128)(2,1)}), bf16[8,128,512]{1,2,0:T(8,128)(2,1)S(1)}, u32[]{:S(2)}, u32[]{:S(2)}) async-start(bf16[8,128,512]{1,2,0:T(8,128)(2,1)} %bitcast.240), calls=%async_computation.8 | async-start | bytes 2097152 | tf_op jit(solution)/shard_map/cond/branch_4_fun/all_to_all | solution.py:41
  168.6 8.0 %broadcast_select_fusion.12 = (bf16[32,65536]{1,0:T(8,128)(2,1)}, bf16[32,65536]{1,0:T(8,128)(2,1)}) fusion(bf16[32,65536]{1,0:T(8,128)(2,1)} %get-tuple-element.1188, bf16[32,65536]{1,0:T(8,128)(2,1)} %get-tuple-element.1357, pred[32]{0:T(512)(128)(4,1)S(1)} %get-tuple-element.1329, bf16[32,65536]{1,0:T(8,128)(2,1)} %get-tuple-element.1170, ...), kind=kLoop, calls=%fused_computation.165 | loop fusion | flops 4194304 | bytes 20971584 | tf_op jit(solution)/shard_map/jit(_take)/select_n | solution.py:77
  176.6 10.4 %reshape.428 = bf16[8,4,1024,64]{3,2,1,0:T(8,128)(2,1)} reshape(bf16[32,65536]{1,0:T(8,128)(2,1)} %get-tuple-element.1328) | data formatting | bytes 8388608 | tf_op jit(solution)/shard_map/cond/branch_4_fun/reshape | solution.py:111
  187.0 8.5 %copy.161 = bf16[8,4,1024,64]{2,3,1,0:T(8,128)(2,1)} copy(bf16[8,4,1024,64]{3,2,1,0:T(8,128)(2,1)} %reshape.428) | data formatting | bytes 8388608 | tf_op jit(solution)/shard_map/cond/branch_4_fun/reshape | solution.py:111
  195.6 10.4 %reshape.429 = bf16[32,1024,64]{2,1,0:T(8,128)(2,1)} reshape(bf16[32,65536]{1,0:T(8,128)(2,1)} %get-tuple-element.1327) | data formatting | bytes 8388608 | tf_op jit(solution)/shard_map/cond/branch_4_fun/reshape | solution.py:121
  206.0 8.5 %copy.162 = bf16[32,1024,64]{1,2,0:T(8,128)(2,1)} copy(bf16[32,1024,64]{2,1,0:T(8,128)(2,1)} %reshape.429) | data formatting | bytes 8388608 | tf_op jit(solution)/shard_map/cond/branch_4_fun/reshape | solution.py:121
  214.7 3.6 %fusion.100 = f32[8,128,256]{1,2,0:S(1)} fusion(bf16[8,1024,256]{1,2,0:T(8,128)(2,1)} %bitcast.226, bf16[8,128,1024]{1,2,0:T(8,128)(2,1)S(1)} %get-tuple-element.1121), kind=kOutput, calls=%fused_computation.299 | convolution fusion | flops 536870912 | bytes 7340032 | tf_op jit(solution)/shard_map/cond
  218.4 10.0 %collective-permute-done.8 = bf16[768,1024]{1,0:T(8,128)(2,1)} collective-permute-done((bf16[768,1024]{1,0:T(8,128)(2,1)}, bf16[768,1024]{1,0:T(8,128)(2,1)}, u32[]{:S(2)}, u32[]{:S(2)}) %collective-permute-start.8) | collective-permute-done | bytes 1572896 | tf_op jit(solution)/shard_map/cond/branch_4_fun/ppermute | solution.py:103
  228.4 5.0 %fusion.99 = f32[768,2048]{0,1:S(1)} fusion(bf16[768,1024]{1,0:T(8,128)(2,1)} %collective-permute-done.8, bf16[1024,2048]{0,1:T(8,128)(2,1)S(1)} %bitcast.230), kind=kOutput, calls=%fused_computation.298 | convolution fusion | flops 3221225472 | bytes 12058624 | tf_op jit(solution)/shard_map/cond
  234.3 11.0 %collective-permute-done.9 = f32[768,64]{0,1:T(8,128)S(1)} collective-permute-done((f32[768,64]{0,1:T(8,128)S(1)}, f32[768,64]{0,1:T(8,128)S(1)}, u32[]{:S(2)}, u32[]{:S(2)}) %collective-permute-start.9) | collective-permute-done | bytes 196640 | tf_op jit(solution)/shard_map/cond/branch_4_fun/ppermute | solution.py:139
  247.4 3.5 %all-to-all-start.9 = ((f32[8,128,64]{1,2,0:T(8,128)}), f32[8,128,64]{1,2,0:T(8,128)S(1)}, u32[]{:S(2)}, u32[]{:S(2)}) async-start(f32[8,128,64]{1,2,0:T(8,128)} %bitcast_add_fusion.4), calls=%async_computation.9 | async-start | bytes 524288 | tf_op jit(solution)/shard_map/cond/branch_4_fun/all_to_all | solution.py:41
  251.9 5.1 %all-to-all-done.9 = f32[8,128,64]{1,2,0:T(8,128)S(1)} async-done(((f32[8,128,64]{1,2,0:T(8,128)}), f32[8,128,64]{1,2,0:T(8,128)S(1)}, u32[]{:S(2)}, u32[]{:S(2)}) %all-to-all-start.9) | async-done | bytes 262176 | tf_op jit(solution)/shard_map/cond/branch_4_fun/all_to_all | solution.py:41
  (118 shorter events, 42.9 us)
Async XLA Ops:
  0.0 43.9 %copy-start = (s32[1024]{0:T(1024)S(1)}, s32[1024]{0:T(1024)}, u32[]{:S(2)}) copy-start(s32[1024]{0:T(1024)} %param.18) | copy-start | bytes 12292
  45.2 37.9 %copy-start.25 = (s32[32,4]{1,0:T(8,128)}, s32[32,4]{1,0:T(8,128)S(1)}, u32[]{:S(2)}) copy-start(s32[32,4]{1,0:T(8,128)S(1)} %get-tuple-element.1336) | copy-start | bytes 1540
  45.2 4.4 %copy-start.20 = (pred[16,4]{1,0:T(8,128)(4,1)}, pred[16,4]{1,0:T(8,128)(4,1)S(1)}, u32[]{:S(2)}) copy-start(pred[16,4]{1,0:T(8,128)(4,1)S(1)} %get-tuple-element.1335) | copy-start | bytes 196
  49.5 5.0 %copy-start.16 = (bf16[128,8192]{1,0:T(8,128)(2,1)S(1)}, bf16[128,8192]{1,0:T(8,128)(2,1)}, u32[]{:S(2)}) copy-start(bf16[128,8192]{1,0:T(8,128)(2,1)} %param.15) | copy-start | bytes 6291460
  50.9 18.0 %all-to-all-start.13 = ((bf16[16,4,4096]{2,1,0:T(4,128)(2,1)}), bf16[16,4,4096]{2,1,0:T(4,128)(2,1)S(1)}, u32[]{:S(2)}, u32[]{:S(2)}) async-start(bf16[16,4,4096]{2,1,0:T(4,128)(2,1)} %select_select_fusion), calls=%async_computation.13 | async-start | bytes 1048576 | tf_op jit(solution)/shard_map/all_to_all | solution.py:71
  69.7 48.7 %all-to-all-start.12 = ((bf16[8,128,1024]{1,2,0:T(8,128)(2,1)}), bf16[8,128,1024]{1,2,0:T(8,128)(2,1)S(1)}, u32[]{:S(2)}, u32[]{:S(2)}) async-start(bf16[8,128,1024]{1,2,0:T(8,128)(2,1)} %bitcast.201), calls=%async_computation.12 | async-start | bytes 4194304 | tf_op jit(solution)/shard_map/all_to_all | solution.py:41
  73.3 45.1 %collective-permute-start.12 = (bf16[512,512]{1,0:T(8,128)(2,1)}, bf16[512,512]{1,0:T(8,128)(2,1)S(1)}, u32[]{:S(2)}, u32[]{:S(2)}) collective-permute-start(bf16[512,512]{1,0:T(8,128)(2,1)} %param.21), channel_id=1, source_target_pairs={{0,0},{2,1},{4,2},{6,3},{8,4},{10,5},{12,6},{14,7},{1,8},{3,9},{5,... | collective-permute-start | bytes 1572872 | tf_op jit(solution)/shard_map/ppermute | solution.py:61
  75.0 43.4 %collective-permute-start.13 = (bf16[512,512]{1,0:T(8,128)(2,1)}, bf16[512,512]{1,0:T(8,128)(2,1)S(1)}, u32[]{:S(2)}, u32[]{:S(2)}) collective-permute-start(bf16[512,512]{1,0:T(8,128)(2,1)} %param.21), channel_id=1, source_target_pairs={{1,0},{3,1},{5,2},{7,3},{9,4},{11,5},{13,6},{15,7},{0,8},{2,9},{4,... | collective-permute-start | bytes 1572872 | tf_op jit(solution)/shard_map/ppermute | solution.py:62
  83.2 28.8 %copy-start.59 = (s32[32]{0:T(128)}, s32[32]{0:T(128)S(1)}, u32[]{:S(2)}) copy-start(s32[32]{0:T(128)S(1)} %broadcast_in_dim.486) | copy-start | bytes 388
  83.4 13.7 %copy-start.26 = (s32[32]{0:T(128)}, s32[32]{0:T(128)S(1)}, u32[]{:S(2)}) copy-start(s32[32]{0:T(128)S(1)} %get-tuple-element.1339) | copy-start | bytes 388
  97.1 14.8 %copy-start.60 = (s32[1,4]{1,0:T(1,128)S(1)}, s32[1,4]{1,0:T(1,128)}, u32[]{:S(2)}) copy-start(s32[1,4]{1,0:T(1,128)} %param.17) | copy-start | bytes 52
  121.8 143.7 %copy-start.19 = (bf16[256,512]{1,0:T(8,128)(2,1)S(1)}, bf16[256,512]{1,0:T(8,128)(2,1)}, u32[]{:S(2)}) copy-start(bf16[256,512]{1,0:T(8,128)(2,1)} %reshape.447) | copy-start | bytes 786436
  156.4 72.0 %collective-permute-start.8 = (bf16[768,1024]{1,0:T(8,128)(2,1)}, bf16[768,1024]{1,0:T(8,128)(2,1)}, u32[]{:S(2)}, u32[]{:S(2)}) collective-permute-start(bf16[768,1024]{1,0:T(8,128)(2,1)} %fusion.58), channel_id=1, source_target_pairs={{0,8},{1,9},{2,10},{3,11},{4,12},{5,13},{6,14},{7,15},{8,0},{9,1},... | collective-permute-start | bytes 4718600 | tf_op jit(solution)/shard_map/cond/branch_4_fun/ppermute | solution.py:103
  163.6 5.0 %copy-start.31 = (s32[32]{0:T(128)S(1)}, s32[32]{0:T(128)}, u32[]{:S(2)}) copy-start(s32[32]{0:T(128)} %get-tuple-element.1273) | copy-start | bytes 388 | tf_op jit(solution)/shard_map/cond
  163.6 5.0 %copy-start.38 = (s32[32]{0:T(128)S(1)}, s32[32]{0:T(128)}, u32[]{:S(2)}) copy-start(s32[32]{0:T(128)} %get-tuple-element.1249) | copy-start | bytes 388 | tf_op jit(solution)/shard_map/cond
  163.6 5.0 %copy-start.45 = (s32[32]{0:T(128)S(1)}, s32[32]{0:T(128)}, u32[]{:S(2)}) copy-start(s32[32]{0:T(128)} %get-tuple-element.1393) | copy-start | bytes 388 | tf_op jit(solution)/shard_map/cond
  164.8 82.6 %all-to-all-start.8 = ((bf16[8,128,512]{1,2,0:T(8,128)(2,1)}), bf16[8,128,512]{1,2,0:T(8,128)(2,1)S(1)}, u32[]{:S(2)}, u32[]{:S(2)}) async-start(bf16[8,128,512]{1,2,0:T(8,128)(2,1)} %bitcast.240), calls=%async_computation.8 | async-start | bytes 2097152 | tf_op jit(solution)/shard_map/cond/branch_4_fun/all_to_all | solution.py:41
  186.9 8.6 %copy-start.23 = (pred[1024,32]{0,1:T(8,128)(4,1)S(1)}, pred[1024,32]{0,1:T(8,128)(4,1)}, u32[]{:S(2)}) copy-start(pred[1024,32]{0,1:T(8,128)(4,1)} %get-tuple-element.1304) | copy-start | bytes 98308 | tf_op jit(solution)/shard_map/cond
  186.9 8.6 %copy-start.49 = (pred[32]{0:T(512)(128)(4,1)S(1)}, pred[32]{0:T(512)(128)(4,1)}, u32[]{:S(2)}) copy-start(pred[32]{0:T(512)(128)(4,1)} %reshape.426) | copy-start | bytes 100 | tf_op jit(solution)/shard_map/cond
  206.0 8.6 %copy-start.54 = (s32[32]{0:T(128)S(1)}, s32[32]{0:T(128)}, u32[]{:S(2)}) copy-start(s32[32]{0:T(128)} %get-tuple-element.1291) | copy-start | bytes 388 | tf_op jit(solution)/shard_map/cond
  214.7 13.6 %copy-start.12 = (bf16[32,1024,64]{1,2,0:T(8,128)(2,1)S(1)}, bf16[32,1024,64]{1,2,0:T(8,128)(2,1)}, u32[]{:S(2)}) copy-start(bf16[32,1024,64]{1,2,0:T(8,128)(2,1)} %copy.162) | copy-start | bytes 12582916 | tf_op jit(solution)/shard_map/cond
  234.1 11.3 %collective-permute-start.9 = (f32[768,64]{0,1:T(8,128)S(1)}, f32[768,64]{0,1:T(8,128)S(1)}, u32[]{:S(2)}, u32[]{:S(2)}) collective-permute-start(f32[768,64]{0,1:T(8,128)S(1)} %select_reduce_fusion.20), channel_id=1, source_target_pairs={{0,8},{1,9},{2,10},{3,11},{4,12},{5,13},{6,14},{7,15},{8,0},{9,1},... | collective-permute-start | bytes 589832 | tf_op jit(solution)/shard_map/cond/branch_4_fun/ppermute | solution.py:139
  247.4 9.6 %all-to-all-start.9 = ((f32[8,128,64]{1,2,0:T(8,128)}), f32[8,128,64]{1,2,0:T(8,128)S(1)}, u32[]{:S(2)}, u32[]{:S(2)}) async-start(f32[8,128,64]{1,2,0:T(8,128)} %bitcast_add_fusion.4), calls=%async_computation.9 | async-start | bytes 524288 | tf_op jit(solution)/shard_map/cond/branch_4_fun/all_to_all | solution.py:41
  264.7 2.6 copy-start.1
  (4 other events, 4.8 us)
